TPU v7x, 256 devices: a whole 4x4x8 slice. The times are simulated.
256 devices in a mesh: seq: 32 (over z, y), ch: 8 (over x, core).
Axes of the slice: x: 4, y: 4, z: 8, core: 2. Of those that a mesh axis runs over, the one named last changes fastest.
Arguments:
- q_proj: bfloat16 [16384, 4096], P('seq', 'ch'), may hold values from -6 to 6
- k_proj: bfloat16 [16384, 4096], P('seq', 'ch'), may hold values from -6 to 6
- v_proj: bfloat16 [16384, 4096], P('seq', 'ch'), may hold values from -6 to 6
- short_weight: float32 [3, 3, 4096], P(None, None, 'ch'), may hold values from -3 to 3
- long_filter: bfloat16 [16384, 4096], P('seq', 'ch'), may hold values from -0.046875 to 0.046875
- long_bias: float32 [4096], P('ch'), may hold values from -4 to 4
- residual: bfloat16 [16384, 4096], P('seq', 'ch'), may hold values from -400 to 400
- norm_gain: float32 [4096], P('ch'), may hold values from 0.1 to 1.9
Outputs:
- stream: bfloat16 [16384, 4096], P('seq', 'ch')
- normed: bfloat16 [16384, 4096], P('seq', 'ch')
All inputs are finite; a program needn't handle non-finite values.
Results may differ from a plain program's by a relative error of at most 0.011.
Values may be sent and summed in bfloat16 or wider, within the bound.
A program may use at most 128 MiB of HBM per device.

v0:
```python
import functools
import math

import jax
import jax.numpy as jnp
import ml_dtypes
import numpy as np
from jax import lax
from jax.experimental import pallas as pl
from jax.experimental.pallas import tpu as pltpu
from jax.sharding import PartitionSpec as P

D = 4096
MESH = pl.DeviceIdType.MESH
F32 = jnp.float32
BF16 = jnp.bfloat16
LANES = 128


def tables(pieces):
    n = LANES
    quarter = np.arange(n) + 0.25
    per = n // pieces
    rows = np.array([per * (r % pieces) + r // pieces for r in range(n)])
    angle = 2 * math.pi / n * (quarter[:, None] * rows[None, :] % n)
    first = np.concatenate([np.cos(angle), -np.sin(angle)], axis=0)
    last = np.concatenate([np.cos(angle.T), -np.sin(angle.T)], axis=1) / (n * n)
    points = np.arange(n)
    angle = 2 * math.pi / n * (points[:, None] * points[None, :] % n)
    cosine, sine = np.cos(angle), np.sin(angle)
    second = np.block([[cosine, -sine], [sine, cosine]])
    angle = 2 * math.pi / (n * n) * (quarter[:, None] * points[None, :])
    return (
        first.astype(ml_dtypes.bfloat16),
        second.astype(ml_dtypes.bfloat16),
        second.T.copy().astype(ml_dtypes.bfloat16),
        last.astype(ml_dtypes.bfloat16),
        np.cos(angle).astype(np.float32),
        np.sin(angle).astype(np.float32),
    )


def dot(left, right):
    return jnp.dot(left, right, preferred_element_type=F32)


def kernel(
    pieces,
    groups,
    q_in, k_in, v_in, h_in, res_in, taps_in, bias_in, gain_in,
    first_in, second_in, third_in, last_in, cos_in, sin_in,
    stream_out, normed_out,
    q_b, k_b, v_b, h_b, res_b, taps, bias, gain,
    first, second, third, last, cos_t, sin_t,
    pad_q, pad_k, pad_v, halo_out, halo_in,
    h_send, z_send, y_send, h_recv, z_recv, y_recv,
    gate_t, skip_t, res_t, flat, spectrum_h, product, power_slots, normed_b, stream_b,
    load_sem, halo_sem, send_sem, recv_sem, power_sem, store_sem,
):
    me, ch = lax.axis_index("seq"), lax.axis_index("ch")
    tokens, channels = h_b.shape
    own = channels // pieces
    blocks = tokens // LANES
    wide = channels // LANES

    barrier = pltpu.get_barrier_semaphore()

    def greet(d, _):
        pl.semaphore_signal(barrier, inc=1, device_id=(lax.rem(me + d, pieces), ch), device_id_type=MESH)
        return 0

    lax.fori_loop(1, pieces, greet, 0)

    def greet_row(d, _):
        pl.semaphore_signal(barrier, inc=1, device_id=(me, lax.rem(ch + d, groups)), device_id_type=MESH)
        return 0

    lax.fori_loop(1, groups, greet_row, 0)

    pairs = [
        (h_in, h_b), (q_in, q_b), (k_in, k_b), (v_in, v_b), (taps_in, taps), (bias_in, bias), (first_in, first),
        (second_in, second), (third_in, third), (last_in, last), (cos_in, cos_t), (sin_in, sin_t),
        (res_in, res_b), (gain_in, gain),
    ]
    loads = [pltpu.make_async_copy(src, dst, load_sem.at[i]) for i, (src, dst) in enumerate(pairs)]
    for load in loads:
        load.start()

    loads[0].wait()
    for r in range(blocks):
        for c in range(wide):
            tile = h_b[r * LANES : (r + 1) * LANES, c * LANES : (c + 1) * LANES]
            h_send[c * LANES : (c + 1) * LANES, r * LANES : (r + 1) * LANES] = tile.T

    for i in (1, 2, 3):
        loads[i].wait()
    tails = [x[tokens - 16 :, :].astype(F32)[14:, :] for x in (q_b, k_b, v_b)]
    halo_out[...] = jnp.concatenate(tails + [jnp.zeros((2, channels), F32)], axis=0)

    pl.semaphore_wait(barrier, pieces - 1 + groups - 1)

    halo_copy = pltpu.make_async_remote_copy(
        src_ref=halo_out, dst_ref=halo_in, send_sem=halo_sem.at[0], recv_sem=halo_sem.at[1],
        device_id=(lax.rem(me + 1, pieces), ch), device_id_type=MESH,
    )

    @pl.when(me < pieces - 1)
    def _():
        halo_copy.start()

    def send_all(source, target, slot):
        def send(d, _):
            other = lax.rem(me + d, pieces)
            pltpu.make_async_remote_copy(
                src_ref=source.at[pl.ds(pl.multiple_of(other * own, own), own)],
                dst_ref=target.at[pl.ds(pl.multiple_of(me * own, own), own)],
                send_sem=send_sem.at[slot], recv_sem=recv_sem.at[slot],
                device_id=(other, ch), device_id_type=MESH,
            ).start()
            return 0

        lax.fori_loop(1, pieces, send, 0)
        mine = pl.ds(pl.multiple_of(me * own, own), own)
        pltpu.make_async_copy(source.at[mine], target.at[mine], recv_sem.at[slot]).start()

    def wait_recv(target, slot):
        pltpu.make_async_copy(target, target, recv_sem.at[slot]).wait()

    def wait_send(source, slot):
        part = source.at[pl.ds(0, channels - own)]
        pltpu.make_async_copy(part, part, send_sem.at[slot]).wait()

    send_all(h_send, h_recv, 0)

    @pl.when(me == 0)
    def _():
        halo_in[...] = jnp.zeros_like(halo_in)

    for x, padded in ((q_b, pad_q), (k_b, pad_k), (v_b, pad_v)):
        padded[8:, :] = x[...].astype(F32)

    @pl.when(me > 0)
    def _():
        halo_copy.wait_recv()

    @pl.when(me < pieces - 1)
    def _():
        halo_copy.wait_send()

    for i, padded in enumerate((pad_q, pad_k, pad_v)):
        padded[6:8, :] = halo_in[2 * i : 2 * i + 2, :]

    for i in (4, 5):
        loads[i].wait()

    for r in range(blocks):
        for c in range(wide):
            cols = slice(c * LANES, (c + 1) * LANES)
            rows = slice(r * LANES, (r + 1) * LANES)

            def short(s, padded):
                total = taps[s, 0:1, cols] * padded[8 + r * LANES : 8 + (r + 1) * LANES, cols]
                total += taps[s, 1:2, cols] * padded[7 + r * LANES : 7 + (r + 1) * LANES, cols]
                return total + taps[s, 2:3, cols] * padded[6 + r * LANES : 6 + (r + 1) * LANES, cols]

            pregate = (short(1, pad_k) * short(2, pad_v)).astype(BF16)
            z_send[cols, rows] = pregate.T
            gate_t[cols, rows] = short(0, pad_q).T
            skip_t[cols, rows] = (pregate.astype(F32) * bias[0:1, cols]).T

    send_all(z_send, z_recv, 1)

    loads[12].wait()
    for r in range(blocks):
        for c in range(wide):
            cols = slice(c * LANES, (c + 1) * LANES)
            rows = slice(r * LANES, (r + 1) * LANES)
            res_t[cols, rows] = res_b[rows, cols].T.astype(F32)

    for i in (6, 7, 8, 9, 10, 11, 13):
        loads[i].wait()

    def forward(received, p):
        signal = [
            jnp.concatenate(
                [flat[i, pl.ds(2 * p + e, pieces, stride=own), :] for i in range(blocks)], axis=0
            )
            for e in range(2)
        ]
        signal = jnp.concatenate(signal, axis=1).astype(BF16)
        partial = dot(first[...], signal)
        turned = []
        for e in range(2):
            real = partial[:LANES, e * LANES : (e + 1) * LANES]
            imag = partial[LANES:, e * LANES : (e + 1) * LANES]
            cosine, sine = cos_t[...], sin_t[...]
            turned.append(
                jnp.concatenate([real * cosine + imag * sine, imag * cosine - real * sine], axis=1).astype(BF16)
            )
        return dot(jnp.concatenate(turned, axis=0), second[...])

    def widen(received):
        def step(r, _):
            rows = pl.ds(pl.multiple_of(r * 64, 64), 64)
            for i in range(blocks):
                flat[i, rows, :] = received[rows, i * LANES : (i + 1) * LANES].astype(F32)
            return 0

        lax.fori_loop(0, channels // 64, step, 0)

    wait_recv(h_recv, 0)
    widen(h_recv)

    def filter_step(p, _):
        spectrum_h[pl.ds(pl.multiple_of(p * 256, 256), 256), :] = forward(h_recv, p)
        return 0

    lax.fori_loop(0, own // 2, filter_step, 0)

    wait_recv(z_recv, 1)
    widen(z_recv)

    def signal_step(p, _):
        x = forward(z_recv, p)
        w = spectrum_h[pl.ds(pl.multiple_of(p * 256, 256), 256), :]
        xr, xi, wr, wi = x[:, :LANES], x[:, LANES:], w[:, :LANES], w[:, LANES:]
        both = jnp.concatenate([xr * wr - xi * wi, xr * wi + xi * wr], axis=1).astype(BF16)
        back = dot(both, third[...])
        turned = []
        for e in range(2):
            real = back[e * LANES : (e + 1) * LANES, :LANES]
            imag = back[e * LANES : (e + 1) * LANES, LANES:]
            cosine, sine = cos_t[...], sin_t[...]
            turned.append(
                jnp.concatenate([real * cosine - imag * sine, real * sine + imag * cosine], axis=0).astype(BF16)
            )
        result = dot(last[...], jnp.concatenate(turned, axis=1))
        for e in range(2):
            for i in range(blocks):
                product[i, pl.ds(2 * p + e, pieces, stride=own), :] = result[
                    i * pieces : (i + 1) * pieces, e * LANES : (e + 1) * LANES
                ]
        return 0

    lax.fori_loop(0, own // 2, signal_step, 0)

    def narrow(r, _):
        rows = pl.ds(pl.multiple_of(r * 64, 64), 64)
        for i in range(blocks):
            y_send[rows, i * LANES : (i + 1) * LANES] = product[i, rows, :].astype(BF16)
        return 0

    lax.fori_loop(0, channels // 64, narrow, 0)
    send_all(y_send, y_recv, 2)

    wait_recv(y_recv, 2)

    def gate_step(r, total):
        rows = pl.ds(pl.multiple_of(r * 32, 32), 32)
        mixed = (gate_t[rows, :] * (y_recv[rows, :].astype(F32) + skip_t[rows, :])).astype(BF16)
        stream = (res_t[rows, :] + mixed.astype(F32)).astype(BF16).astype(F32)
        res_t[rows, :] = stream
        squares = stream * stream
        return total + ((squares[0:8] + squares[8:16]) + (squares[16:24] + squares[24:32]))

    total = lax.fori_loop(0, channels // 32, gate_step, jnp.zeros((8, tokens), F32))
    power_slots[ch] = jnp.sum(total, axis=0, keepdims=True)

    def power_copy(d):
        other = lax.rem(ch + d, groups)
        return pltpu.make_async_remote_copy(
            src_ref=power_slots.at[ch], dst_ref=power_slots.at[ch],
            send_sem=power_sem.at[0], recv_sem=power_sem.at[1],
            device_id=(me, other), device_id_type=MESH,
        )

    for d in range(1, groups):
        power_copy(d).start()

    for r in range(blocks):
        for c in range(wide):
            cols = slice(c * LANES, (c + 1) * LANES)
            rows = slice(r * LANES, (r + 1) * LANES)
            stream_b[rows, cols] = res_t[cols, rows].T.astype(BF16)
    stream_copy = pltpu.make_async_copy(stream_b, stream_out, store_sem.at[0])
    stream_copy.start()

    part = power_slots.at[pl.ds(0, groups - 1)]
    pltpu.make_async_copy(part, part, power_sem.at[1]).wait()
    power = jnp.sum(power_slots[...], axis=0) / D
    scale = lax.rsqrt(power + 1e-6)
    for r in range(blocks):
        rows = slice(r * LANES, (r + 1) * LANES)
        column = jnp.broadcast_to(scale[:, rows], (LANES, LANES)).T
        for c in range(wide):
            cols = slice(c * LANES, (c + 1) * LANES)
            normed_b[rows, cols] = (stream_b[rows, cols].astype(F32) * column * gain[0:1, cols]).astype(BF16)
    normed_copy = pltpu.make_async_copy(normed_b, normed_out, store_sem.at[1])
    normed_copy.start()

    pltpu.make_async_copy(part, part, power_sem.at[0]).wait()
    wait_send(h_send, 0)
    wait_send(z_send, 1)
    wait_send(y_send, 2)
    stream_copy.wait()
    normed_copy.wait()


def per_device(constants, q_proj, k_proj, v_proj, short_weight, long_filter, long_bias, residual, norm_gain):
    tokens, channels = q_proj.shape
    pieces, groups = lax.axis_size("seq"), lax.axis_size("ch")
    own = channels // pieces
    block = (tokens, channels)
    operands = (
        q_proj, k_proj, v_proj, long_filter, residual, short_weight,
        long_bias.reshape(1, channels), norm_gain.reshape(1, channels),
    ) + constants
    scratch = [pltpu.VMEM(block, BF16) for _ in range(5)]
    scratch += [pltpu.VMEM(x.shape, x.dtype) for x in operands[5:]]
    scratch += [pltpu.VMEM((tokens + 8, channels), F32) for _ in range(3)]
    scratch += [pltpu.VMEM((8, channels), F32) for _ in range(2)]
    scratch += [pltpu.VMEM((channels, tokens), BF16) for _ in range(6)]
    scratch += [pltpu.VMEM((channels, tokens), F32) for _ in range(3)]
    scratch += [
        pltpu.VMEM((tokens // LANES, channels, LANES), F32),
        pltpu.VMEM((own * LANES, 2 * LANES), F32),
        pltpu.VMEM((tokens // LANES, channels, LANES), F32),
        pltpu.VMEM((groups, 1, tokens), F32),
        pltpu.VMEM(block, BF16),
        pltpu.VMEM(block, BF16),
    ]
    scratch += [pltpu.SemaphoreType.DMA((count,)) for count in (14, 2, 3, 3, 2, 2)]
    anywhere = pl.BlockSpec(memory_space=pl.ANY)
    return pl.pallas_call(
        functools.partial(kernel, pieces, groups),
        out_shape=(jax.ShapeDtypeStruct(block, BF16),) * 2,
        in_specs=[anywhere] * len(operands),
        out_specs=(anywhere,) * 2,
        scratch_shapes=scratch,
        compiler_params=pltpu.CompilerParams(
            collective_id=0, has_side_effects=True, vmem_limit_bytes=48 * 2**20
        ),
        cost_estimate=pl.CostEstimate(flops=1_300_000_000, bytes_accessed=4_000_000, transcendentals=0),
    )(*operands)


def solution(mesh):
    pieces = mesh.shape["seq"]
    constants = tuple(jnp.asarray(x) for x in tables(pieces))
    placed = (
        P("seq", "ch"),
        P("seq", "ch"),
        P("seq", "ch"),
        P(None, None, "ch"),
        P("seq", "ch"),
        P("ch"),
        P("seq", "ch"),
        P("ch"),
    )
    return jax.shard_map(
        functools.partial(per_device, constants),
        mesh=mesh,
        in_specs=placed,
        out_specs=(P("seq", "ch"), P("seq", "ch")),
        check_vma=False,
    )
```

profile of v0, /device:TPU:1, one launch (start us, length us, event | category | flops | bytes accessed | tf_op | source)
XLA Modules:
  0.0 74.8 jit_solution(14395938939347365665)
XLA Ops:
  0.6 0.0 copy-start.6
  0.6 0.7 copy-done.6
  1.3 0.0 copy-start
  1.3 1.0 %copy-done = bf16[512,512]{1,0:T(8,128)(2,1)S(1)} copy-done((bf16[512,512]{1,0:T(8,128)(2,1)S(1)}, bf16[512,512]{1,0:T(8,128)(2,1)}, u32[]{:S(2)}) %copy-start) | copy-done | bytes 524312
  2.4 0.0 copy-start.1
  2.4 1.0 %copy-done.1 = bf16[512,512]{1,0:T(8,128)(2,1)S(1)} copy-done((bf16[512,512]{1,0:T(8,128)(2,1)S(1)}, bf16[512,512]{1,0:T(8,128)(2,1)}, u32[]{:S(2)}) %copy-start.1) | copy-done | bytes 524312
  3.4 0.0 copy-start.2
  3.4 1.0 %copy-done.2 = bf16[512,512]{1,0:T(8,128)(2,1)S(1)} copy-done((bf16[512,512]{1,0:T(8,128)(2,1)S(1)}, bf16[512,512]{1,0:T(8,128)(2,1)}, u32[]{:S(2)}) %copy-start.2) | copy-done | bytes 524312
  4.4 0.0 copy-start.3
  4.4 1.0 %copy-done.3 = bf16[512,512]{1,0:T(8,128)(2,1)S(1)} copy-done((bf16[512,512]{1,0:T(8,128)(2,1)S(1)}, bf16[512,512]{1,0:T(8,128)(2,1)}, u32[]{:S(2)}) %copy-start.3) | copy-done | bytes 524312
  5.5 0.0 copy-start.4
  5.5 1.0 %copy-done.4 = bf16[512,512]{1,0:T(8,128)(2,1)S(1)} copy-done((bf16[512,512]{1,0:T(8,128)(2,1)S(1)}, bf16[512,512]{1,0:T(8,128)(2,1)}, u32[]{:S(2)}) %copy-start.4) | copy-done | bytes 524312
  6.5 0.0 copy-start.5
  6.5 0.7 copy-done.5
  7.3 0.0 copy-start.7
  7.3 0.7 copy-done.7
  7.9 0.0 copy-start.8
  7.9 0.9 %copy-done.8 = bf16[256,256]{1,0:T(8,128)(2,1)S(1)} copy-done((bf16[256,256]{1,0:T(8,128)(2,1)S(1)}, bf16[256,256]{1,0:T(8,128)(2,1)}, u32[]{:S(2)}) %copy-start.8) | copy-done | bytes 131096
  8.9 0.0 copy-start.9
  8.9 0.9 %copy-done.9 = bf16[256,256]{1,0:T(8,128)(2,1)S(1)} copy-done((bf16[256,256]{1,0:T(8,128)(2,1)S(1)}, bf16[256,256]{1,0:T(8,128)(2,1)}, u32[]{:S(2)}) %copy-start.9) | copy-done | bytes 131096
  9.8 0.0 copy-start.10
  9.8 0.8 %copy-done.10 = f32[128,128]{1,0:T(8,128)S(1)} copy-done((f32[128,128]{1,0:T(8,128)S(1)}, f32[128,128]{1,0:T(8,128)}, u32[]{:S(2)}) %copy-start.10) | copy-done | bytes 65560
  10.6 0.0 copy-start.11
  10.6 0.8 %copy-done.11 = f32[128,128]{1,0:T(8,128)S(1)} copy-done((f32[128,128]{1,0:T(8,128)S(1)}, f32[128,128]{1,0:T(8,128)}, u32[]{:S(2)}) %copy-start.11) | copy-done | bytes 65560
  11.4 0.0 copy-start.12
  11.4 0.8 %copy-done.12 = bf16[128,256]{1,0:T(8,128)(2,1)S(1)} copy-done((bf16[128,256]{1,0:T(8,128)(2,1)S(1)}, bf16[128,256]{1,0:T(8,128)(2,1)}, u32[]{:S(2)}) %copy-start.12) | copy-done | bytes 65560
  12.3 0.0 copy-start.13
  12.3 0.8 %copy-done.13 = bf16[256,128]{1,0:T(8,128)(2,1)S(1)} copy-done((bf16[256,128]{1,0:T(8,128)(2,1)S(1)}, bf16[256,128]{1,0:T(8,128)(2,1)}, u32[]{:S(2)}) %copy-start.13) | copy-done | bytes 65560
  13.1 60.1 %shard_map.149 = (bf16[512,512]{1,0:T(8,128)(2,1)S(1)}, bf16[512,512]{1,0:T(8,128)(2,1)S(1)}) custom-call(bf16[512,512]{1,0:T(8,128)(2,1)S(1)} %copy-done, bf16[512,512]{1,0:T(8,128)(2,1)S(1)} %copy-done.1, bf16[512,512]{1,0:T(8,128)(2,1)S(1)} %copy-done.2, bf16[512,512]{1,0:T(8,128)(2,1)S(1)} %copy-done.3, bf16[512,512]{1,0:T(8,128)(2,1)S(1)} %copy-done.4, ...), custom_call_target="tpu_custom_call" | custom-call | flops 1300000000 | bytes 4000000 | tf_op jit(solution)/shard_map/pallas_call | solution.py:334
  73.3 0.8 %copy.18 = bf16[512,512]{1,0:T(8,128)(2,1)} copy(bf16[512,512]{1,0:T(8,128)(2,1)S(1)} %get-tuple-element.4) | data formatting | bytes 1048576
  74.1 0.8 %copy.19 = bf16[512,512]{1,0:T(8,128)(2,1)} copy(bf16[512,512]{1,0:T(8,128)(2,1)S(1)} %get-tuple-element.5) | data formatting | bytes 1048576
Async XLA Ops:
  0.6 0.7 copy-start.6
  1.3 1.0 %copy-start = (bf16[512,512]{1,0:T(8,128)(2,1)S(1)}, bf16[512,512]{1,0:T(8,128)(2,1)}, u32[]{:S(2)}) copy-start(bf16[512,512]{1,0:T(8,128)(2,1)} %q_in.1) | copy-start | bytes 1572868
  2.4 1.0 %copy-start.1 = (bf16[512,512]{1,0:T(8,128)(2,1)S(1)}, bf16[512,512]{1,0:T(8,128)(2,1)}, u32[]{:S(2)}) copy-start(bf16[512,512]{1,0:T(8,128)(2,1)} %k_in.1) | copy-start | bytes 1572868
  3.4 1.0 %copy-start.2 = (bf16[512,512]{1,0:T(8,128)(2,1)S(1)}, bf16[512,512]{1,0:T(8,128)(2,1)}, u32[]{:S(2)}) copy-start(bf16[512,512]{1,0:T(8,128)(2,1)} %v_in.1) | copy-start | bytes 1572868
  4.4 1.0 %copy-start.3 = (bf16[512,512]{1,0:T(8,128)(2,1)S(1)}, bf16[512,512]{1,0:T(8,128)(2,1)}, u32[]{:S(2)}) copy-start(bf16[512,512]{1,0:T(8,128)(2,1)} %h_in.1) | copy-start | bytes 1572868
  5.5 1.0 %copy-start.4 = (bf16[512,512]{1,0:T(8,128)(2,1)S(1)}, bf16[512,512]{1,0:T(8,128)(2,1)}, u32[]{:S(2)}) copy-start(bf16[512,512]{1,0:T(8,128)(2,1)} %res_in.1) | copy-start | bytes 1572868
  6.5 0.7 copy-start.5
  7.3 0.7 copy-start.7
  7.9 0.9 %copy-start.8 = (bf16[256,256]{1,0:T(8,128)(2,1)S(1)}, bf16[256,256]{1,0:T(8,128)(2,1)}, u32[]{:S(2)}) copy-start(bf16[256,256]{1,0:T(8,128)(2,1)} %constant.14.clone.third_in) | copy-start | bytes 393220
  8.9 0.9 %copy-start.9 = (bf16[256,256]{1,0:T(8,128)(2,1)S(1)}, bf16[256,256]{1,0:T(8,128)(2,1)}, u32[]{:S(2)}) copy-start(bf16[256,256]{1,0:T(8,128)(2,1)} %constant.13.clone.second_in) | copy-start | bytes 393220
  9.8 0.8 %copy-start.10 = (f32[128,128]{1,0:T(8,128)S(1)}, f32[128,128]{1,0:T(8,128)}, u32[]{:S(2)}) copy-start(f32[128,128]{1,0:T(8,128)} %constant.17.clone.sin_in) | copy-start | bytes 196612
  10.6 0.8 %copy-start.11 = (f32[128,128]{1,0:T(8,128)S(1)}, f32[128,128]{1,0:T(8,128)}, u32[]{:S(2)}) copy-start(f32[128,128]{1,0:T(8,128)} %constant.16.clone.cos_in) | copy-start | bytes 196612
  11.4 0.8 %copy-start.12 = (bf16[128,256]{1,0:T(8,128)(2,1)S(1)}, bf16[128,256]{1,0:T(8,128)(2,1)}, u32[]{:S(2)}) copy-start(bf16[128,256]{1,0:T(8,128)(2,1)} %constant.15.clone.last_in) | copy-start | bytes 196612
  12.3 0.8 %copy-start.13 = (bf16[256,128]{1,0:T(8,128)(2,1)S(1)}, bf16[256,128]{1,0:T(8,128)(2,1)}, u32[]{:S(2)}) copy-start(bf16[256,128]{1,0:T(8,128)(2,1)} %constant.12.clone.first_in) | copy-start | bytes 196612
where the time goes:
time: 75.5 us; the launch traced here: 74.8 us
  Pallas kernels  60.1 us (80%)
  local copies, waits for them, and re-layouts  14 us (19%)
    pallas_call x1, Pallas kernels, per_device(): pl.pallas_call(functools.partial(kernel, pieces, groups), out_shape=(jax....  60.1 us
    unnamed x30, local copies, waits for them, and re-layouts  14 us

commit v1 on v0

v1 whole, which is shorter than its diff:
```python
import functools
import math

import jax
import jax.numpy as jnp
import ml_dtypes
import numpy as np
from jax import lax
from jax.experimental import pallas as pl
from jax.experimental.pallas import tpu as pltpu
from jax.sharding import PartitionSpec as P

D = 4096
MESH = pl.DeviceIdType.MESH
F32 = jnp.float32
BF16 = jnp.bfloat16
LANES = 128


def tables(pieces):
    n = LANES
    quarter = np.arange(n) + 0.25
    per = n // pieces
    rows = np.array([per * (r % pieces) + r // pieces for r in range(n)])
    angle = 2 * math.pi / n * (quarter[:, None] * rows[None, :] % n)
    first = np.concatenate([np.cos(angle), -np.sin(angle)], axis=0)
    last = np.concatenate([np.cos(angle.T), -np.sin(angle.T)], axis=1) / (n * n)
    points = np.arange(n)
    angle = 2 * math.pi / n * (points[:, None] * points[None, :] % n)
    cosine, sine = np.cos(angle), np.sin(angle)
    second = np.block([[cosine, -sine], [sine, cosine]])
    angle = 2 * math.pi / (n * n) * (quarter[:, None] * points[None, :])
    return (
        first.astype(ml_dtypes.bfloat16),
        second.astype(ml_dtypes.bfloat16),
        second.T.copy().astype(ml_dtypes.bfloat16),
        last.astype(ml_dtypes.bfloat16),
        np.cos(angle).astype(np.float32),
        np.sin(angle).astype(np.float32),
    )


def dot(left, right):
    return jnp.dot(left, right, preferred_element_type=F32)


def order(step, count):
    half = (step + 1) // 2
    return lax.rem(count // 2 + jnp.where(lax.rem(step, 2) == 1, -half, half), count)


def kernel(
    pieces,
    groups,
    q_in, k_in, v_in, h_in, res_in, taps_in, bias_in, gain_in,
    first_in, second_in, third_in, last_in, cos_in, sin_in,
    stream_out, normed_out,
    q_b, k_b, v_b, h_b, res_b, taps, bias, gain,
    first, second, third, last, cos_t, sin_t,
    pad_q, pad_k, pad_v, halo_out, halo_in,
    h_send, h_recv, z_send, z_recv, y_send, y_recv, pregate_b,
    gate_t, skip_t, res_t, flat, spectrum_h, product, power_slots, normed_b, stream_b,
    load_sem, halo_sem, send_sem, recv_sem, power_sem, store_sem,
):
    me, ch = lax.axis_index("seq"), lax.axis_index("ch")
    tokens, channels = h_b.shape
    own = channels // pieces
    blocks = tokens // LANES
    wide = channels // LANES
    line = 4
    rings = pieces // line

    def peer(step):
        z = lax.rem(me // line + order(step // line, rings), rings)
        y = lax.rem(lax.rem(me, line) + order(lax.rem(step, line), line), line)
        return z * line + y

    barrier = pltpu.get_barrier_semaphore()

    def greet(step, _):
        pl.semaphore_signal(barrier, inc=1, device_id=(peer(step), ch), device_id_type=MESH)
        return 0

    lax.fori_loop(0, pieces - 1, greet, 0)

    def greet_row(d, _):
        pl.semaphore_signal(barrier, inc=1, device_id=(me, lax.rem(ch + d, groups)), device_id_type=MESH)
        return 0

    lax.fori_loop(1, groups, greet_row, 0)

    pairs = [
        (h_in, h_b), (q_in, q_b), (k_in, k_b), (v_in, v_b), (taps_in, taps), (bias_in, bias), (first_in, first),
        (second_in, second), (third_in, third), (last_in, last), (cos_in, cos_t), (sin_in, sin_t),
        (res_in, res_b), (gain_in, gain),
    ]
    loads = [pltpu.make_async_copy(src, dst, load_sem.at[i]) for i, (src, dst) in enumerate(pairs)]
    for load in loads:
        load.start()

    def tile(r, c):
        return slice(r * LANES, (r + 1) * LANES), slice(c * LANES, (c + 1) * LANES)

    loads[0].wait()
    for r in range(blocks):
        for c in range(wide):
            rows, cols = tile(r, c)
            h_send[cols, rows] = h_b[rows, cols].T

    for i in (1, 2, 3):
        loads[i].wait()
    tails = [x[tokens - 16 :, :].astype(F32)[14:, :] for x in (q_b, k_b, v_b)]
    halo_out[...] = jnp.concatenate(tails + [jnp.zeros((2, channels), F32)], axis=0)

    pl.semaphore_wait(barrier, pieces - 1 + groups - 1)

    halo_copy = pltpu.make_async_remote_copy(
        src_ref=halo_out, dst_ref=halo_in, send_sem=halo_sem.at[0], recv_sem=halo_sem.at[1],
        device_id=(lax.rem(me + 1, pieces), ch), device_id_type=MESH,
    )

    @pl.when(me < pieces - 1)
    def _():
        halo_copy.start()

    def send_all(source, target, slot):
        def send(step, _):
            other = peer(step)
            pltpu.make_async_remote_copy(
                src_ref=source.at[pl.ds(pl.multiple_of(other * own, own), own)],
                dst_ref=target.at[pl.ds(pl.multiple_of(me * own, own), own)],
                send_sem=send_sem.at[slot], recv_sem=recv_sem.at[slot],
                device_id=(other, ch), device_id_type=MESH,
            ).start()
            return 0

        lax.fori_loop(0, pieces - 1, send, 0)
        mine = pl.ds(pl.multiple_of(me * own, own), own)
        pltpu.make_async_copy(source.at[mine], target.at[mine], recv_sem.at[slot]).start()

    def wait_recv(target, slot):
        pltpu.make_async_copy(target, target, recv_sem.at[slot]).wait()

    def wait_send(source, slot):
        part = source.at[pl.ds(0, channels - own)]
        pltpu.make_async_copy(part, part, send_sem.at[slot]).wait()

    send_all(h_send, h_recv, 0)

    @pl.when(me == 0)
    def _():
        halo_in[...] = jnp.zeros_like(halo_in)

    for x, padded in ((k_b, pad_k), (v_b, pad_v), (q_b, pad_q)):
        padded[8:, :] = x[...].astype(F32)

    @pl.when(me > 0)
    def _():
        halo_copy.wait_recv()

    @pl.when(me < pieces - 1)
    def _():
        halo_copy.wait_send()

    for i, padded in enumerate((pad_q, pad_k, pad_v)):
        padded[6:8, :] = halo_in[2 * i : 2 * i + 2, :]

    for i in (4, 5):
        loads[i].wait()

    def short(s, padded, r, c):
        cols = tile(r, c)[1]
        total = taps[s, 0:1, cols] * padded[8 + r * LANES : 8 + (r + 1) * LANES, cols]
        total += taps[s, 1:2, cols] * padded[7 + r * LANES : 7 + (r + 1) * LANES, cols]
        return total + taps[s, 2:3, cols] * padded[6 + r * LANES : 6 + (r + 1) * LANES, cols]

    half = blocks // 2
    for r in range(half):
        for c in range(wide):
            parts = []
            for e in range(2):
                rows, cols = tile(r + e * half, c)
                pregate = (short(1, pad_k, r + e * half, c) * short(2, pad_v, r + e * half, c)).astype(BF16)
                pregate_b[rows, cols] = pregate
                parts.append(pregate.astype(F32).T.reshape(LANES // own, 2, own // 2, LANES))
            rows, cols = tile(r, c)
            for part in range(2):
                z_send[part, cols, rows] = (
                    jnp.stack([x[:, part] for x in parts], axis=1).reshape(LANES, LANES).astype(BF16)
                )

    for part in range(2):
        send_all(z_send.at[part], z_recv.at[part], 1 + part)

    loads[12].wait()
    for r in range(blocks):
        for c in range(wide):
            rows, cols = tile(r, c)
            gate_t[cols, rows] = short(0, pad_q, r, c).T
            skip_t[cols, rows] = (pregate_b[rows, cols].astype(F32) * bias[0:1, cols]).T
            res_t[cols, rows] = res_b[rows, cols].T.astype(F32)

    for i in (6, 7, 8, 9, 10, 11, 13):
        loads[i].wait()

    def forward(signal):
        partial = dot(first[...], jnp.concatenate(signal, axis=1).astype(BF16))
        turned = []
        for e in range(2):
            real = partial[:LANES, e * LANES : (e + 1) * LANES]
            imag = partial[LANES:, e * LANES : (e + 1) * LANES]
            cosine, sine = cos_t[...], sin_t[...]
            turned.append(
                jnp.concatenate([real * cosine + imag * sine, imag * cosine - real * sine], axis=1).astype(BF16)
            )
        return dot(jnp.concatenate(turned, axis=0), second[...])

    def widen(received, count):
        def step(r, _):
            rows = pl.ds(pl.multiple_of(r * 64, 64), 64)
            for i in range(count):
                flat[i, rows, :] = received[rows, i * LANES : (i + 1) * LANES].astype(F32)
            return 0

        lax.fori_loop(0, channels // 64, step, 0)

    wait_recv(h_recv, 0)
    widen(h_recv, blocks)

    def filter_step(p, _):
        signal = [
            jnp.concatenate([flat[i, pl.ds(2 * p + e, pieces, stride=own), :] for i in range(blocks)], axis=0)
            for e in range(2)
        ]
        spectrum_h[pl.ds(pl.multiple_of(p * 256, 256), 256), :] = forward(signal)
        return 0

    lax.fori_loop(0, own // 2, filter_step, 0)

    for part in range(2):
        wait_recv(z_recv.at[part], 1 + part)
        widen(z_recv.at[part], half)

        def signal_step(p, _):
            signal = [
                jnp.concatenate(
                    [
                        flat[i % half, pl.ds((i // half) * (own // 2) + 2 * p + e, pieces, stride=own), :]
                        for i in range(blocks)
                    ],
                    axis=0,
                )
                for e in range(2)
            ]
            x = forward(signal)
            w = spectrum_h[pl.ds(pl.multiple_of((part * own // 4 + p) * 256, 256), 256), :]
            xr, xi, wr, wi = x[:, :LANES], x[:, LANES:], w[:, :LANES], w[:, LANES:]
            both = jnp.concatenate([xr * wr - xi * wi, xr * wi + xi * wr], axis=1).astype(BF16)
            back = dot(both, third[...])
            turned = []
            for e in range(2):
                real = back[e * LANES : (e + 1) * LANES, :LANES]
                imag = back[e * LANES : (e + 1) * LANES, LANES:]
                cosine, sine = cos_t[...], sin_t[...]
                turned.append(
                    jnp.concatenate([real * cosine - imag * sine, real * sine + imag * cosine], axis=0).astype(BF16)
                )
            result = dot(last[...], jnp.concatenate(turned, axis=1))
            for e in range(2):
                for i in range(blocks):
                    product[i % half, pl.ds((i // half) * (own // 2) + 2 * p + e, pieces, stride=own), :] = result[
                        i * pieces : (i + 1) * pieces, e * LANES : (e + 1) * LANES
                    ]
            return 0

        lax.fori_loop(0, own // 4, signal_step, 0, unroll=2)

        def narrow(r, _):
            rows = pl.ds(pl.multiple_of(r * 64, 64), 64)
            for i in range(half):
                y_send[part, rows, i * LANES : (i + 1) * LANES] = product[i, rows, :].astype(BF16)
            return 0

        lax.fori_loop(0, channels // 64, narrow, 0)
        send_all(y_send.at[part], y_recv.at[part], 3 + part)

    total = jnp.zeros((8, tokens), F32)
    for part in range(2):
        wait_recv(y_recv.at[part], 3 + part)

        def gate_step(j, total):
            conv = y_recv[part, pl.ds(pl.multiple_of(j * own, own), own), :].astype(F32)
            conv = jnp.concatenate([conv[: own // 2], conv[own // 2 :]], axis=1)
            rows = pl.ds(pl.multiple_of(j * own + part * (own // 2), 8), own // 2)
            mixed = (gate_t[rows, :] * (conv + skip_t[rows, :])).astype(BF16)
            stream = (res_t[rows, :] + mixed.astype(F32)).astype(BF16).astype(F32)
            res_t[rows, :] = stream
            return total + stream * stream

        total = lax.fori_loop(0, pieces, gate_step, total, unroll=4)
    power_slots[ch] = jnp.sum(total, axis=0, keepdims=True)

    def power_copy(d):
        other = lax.rem(ch + d, groups)
        return pltpu.make_async_remote_copy(
            src_ref=power_slots.at[ch], dst_ref=power_slots.at[ch],
            send_sem=power_sem.at[0], recv_sem=power_sem.at[1],
            device_id=(me, other), device_id_type=MESH,
        )

    for d in range(1, groups):
        power_copy(d).start()

    for r in range(blocks):
        for c in range(wide):
            rows, cols = tile(r, c)
            stream_b[rows, cols] = res_t[cols, rows].T.astype(BF16)
    stream_copy = pltpu.make_async_copy(stream_b, stream_out, store_sem.at[0])
    stream_copy.start()

    part = power_slots.at[pl.ds(0, groups - 1)]
    pltpu.make_async_copy(part, part, power_sem.at[1]).wait()
    power = jnp.sum(power_slots[...], axis=0) / D
    scale = lax.rsqrt(power + 1e-6)
    for r in range(blocks):
        rows = tile(r, 0)[0]
        column = jnp.broadcast_to(scale[:, rows], (LANES, LANES)).T
        for c in range(wide):
            cols = tile(r, c)[1]
            normed_b[rows, cols] = (stream_b[rows, cols].astype(F32) * column * gain[0:1, cols]).astype(BF16)
    normed_copy = pltpu.make_async_copy(normed_b, normed_out, store_sem.at[1])
    normed_copy.start()

    pltpu.make_async_copy(part, part, power_sem.at[0]).wait()
    wait_send(h_send, 0)
    for part in range(2):
        wait_send(z_send.at[part], 1 + part)
        wait_send(y_send.at[part], 3 + part)
    stream_copy.wait()
    normed_copy.wait()


def per_device(constants, q_proj, k_proj, v_proj, short_weight, long_filter, long_bias, residual, norm_gain):
    tokens, channels = q_proj.shape
    pieces, groups = lax.axis_size("seq"), lax.axis_size("ch")
    own = channels // pieces
    block = (tokens, channels)
    operands = (
        q_proj, k_proj, v_proj, long_filter, residual, short_weight,
        long_bias.reshape(1, channels), norm_gain.reshape(1, channels),
    ) + constants
    scratch = [pltpu.VMEM(block, BF16) for _ in range(5)]
    scratch += [pltpu.VMEM(x.shape, x.dtype) for x in operands[5:]]
    scratch += [pltpu.VMEM((tokens + 8, channels), F32) for _ in range(3)]
    scratch += [pltpu.VMEM((8, channels), F32) for _ in range(2)]
    scratch += [pltpu.VMEM((channels, tokens), BF16) for _ in range(2)]
    scratch += [pltpu.VMEM((2, channels, tokens // 2), BF16) for _ in range(4)]
    scratch += [pltpu.VMEM(block, BF16)]
    scratch += [pltpu.VMEM((channels, tokens), F32) for _ in range(3)]
    scratch += [
        pltpu.VMEM((tokens // LANES, channels, LANES), F32),
        pltpu.VMEM((own * LANES, 2 * LANES), F32),
        pltpu.VMEM((tokens // LANES // 2, channels, LANES), F32),
        pltpu.VMEM((groups, 1, tokens), F32),
        pltpu.VMEM(block, BF16),
        pltpu.VMEM(block, BF16),
    ]
    scratch += [pltpu.SemaphoreType.DMA((count,)) for count in (14, 2, 5, 5, 2, 2)]
    anywhere = pl.BlockSpec(memory_space=pl.ANY)
    return pl.pallas_call(
        functools.partial(kernel, pieces, groups),
        out_shape=(jax.ShapeDtypeStruct(block, BF16),) * 2,
        in_specs=[anywhere] * len(operands),
        out_specs=(anywhere,) * 2,
        scratch_shapes=scratch,
        compiler_params=pltpu.CompilerParams(
            collective_id=0, has_side_effects=True, vmem_limit_bytes=62 * 2**20
        ),
        cost_estimate=pl.CostEstimate(flops=1_300_000_000, bytes_accessed=4_000_000, transcendentals=0),
    )(*operands)


def solution(mesh):
    pieces = mesh.shape["seq"]
    constants = tuple(jnp.asarray(x) for x in tables(pieces))
    placed = (
        P("seq", "ch"),
        P("seq", "ch"),
        P("seq", "ch"),
        P(None, None, "ch"),
        P("seq", "ch"),
        P("ch"),
        P("seq", "ch"),
        P("ch"),
    )
    return jax.shard_map(
        functools.partial(per_device, constants),
        mesh=mesh,
        in_specs=placed,
        out_specs=(P("seq", "ch"), P("seq", "ch")),
        check_vma=False,
    )
```

time: 75.5 us -> 56.9 us (0.75)
  local copies, waits for them, and re-layouts: 14 us -> 2.72 us
  Pallas kernels: 60.1 us -> 53.4 us
    unnamed x30 -> x4, local copies, waits for them, and re-layouts: 14 us -> 2.72 us
    pallas_call x1, Pallas kernels: 60.1 us -> 53.4 us  [per_device(): pl.pallas_call(functools.partial(kernel, pieces, groups), out_shape=(jax....]
where the time goes in v1:
time: 56.9 us; the launch traced here: 56.8 us
  Pallas kernels  53.4 us (94%)
  local copies, waits for them, and re-layouts  2.72 us (5%)
  between operations  0.65 us (1%)
    pallas_call x1, Pallas kernels, per_device(): pl.pallas_call(functools.partial(kernel, pieces, groups), out_shape=(jax....  53.4 us
    unnamed x4, local copies, waits for them, and re-layouts  2.72 us

profile of v1, /device:TPU:1, one launch (start us, length us, event | category | flops | bytes accessed | tf_op | source)
XLA Modules:
  0.0 56.8 jit_solution(12013941988577147811)
XLA Ops:
  0.6 53.4 %shard_map.149 = (bf16[512,512]{1,0:T(8,128)(2,1)}, bf16[512,512]{1,0:T(8,128)(2,1)}) custom-call(bf16[512,512]{1,0:T(8,128)(2,1)} %q_in.1, bf16[512,512]{1,0:T(8,128)(2,1)} %k_in.1, bf16[512,512]{1,0:T(8,128)(2,1)} %v_in.1, bf16[512,512]{1,0:T(8,128)(2,1)} %h_in.1, bf16[512,512]{1,0:T(8,128)(2,1)} %res_in.1, f32[3,3,512]{2,1,0:T(4,128)} %taps_in.1, ...), custom_call_target="tpu_custom_call" | custom-call | flops 1300000000 | bytes 4000000 | tf_op jit(solution)/shard_map/pallas_call | solution.py:370
  54.1 0.0 copy-start
  54.1 1.9 %copy.18 = bf16[512,512]{1,0:T(8,128)(2,1)} copy(bf16[512,512]{1,0:T(8,128)(2,1)} %get-tuple-element.4) | data formatting | bytes 1048576
  56.0 0.0 copy-done
  56.0 0.8 %copy.19 = bf16[512,512]{1,0:T(8,128)(2,1)} copy(bf16[512,512]{1,0:T(8,128)(2,1)S(1)} %copy-done) | data formatting | bytes 1048576
Async XLA Ops:
  54.1 1.9 %copy-start = (bf16[512,512]{1,0:T(8,128)(2,1)S(1)}, bf16[512,512]{1,0:T(8,128)(2,1)}, u32[]{:S(2)}) copy-start(bf16[512,512]{1,0:T(8,128)(2,1)} %get-tuple-element.5) | copy-start | bytes 1572868

commit v2 on v1

--- a/solution.py
+++ b/solution.py
@@ -54,13 +54,13 @@
     groups,
     q_in, k_in, v_in, h_in, res_in, taps_in, bias_in, gain_in,
     first_in, second_in, third_in, last_in, cos_in, sin_in,
-    stream_out, normed_out,
+    stream_b, normed_b,
     q_b, k_b, v_b, h_b, res_b, taps, bias, gain,
     first, second, third, last, cos_t, sin_t,
     pad_q, pad_k, pad_v, halo_out, halo_in,
     h_send, h_recv, z_send, z_recv, y_send, y_recv, pregate_b,
-    gate_t, skip_t, res_t, flat, spectrum_h, product, power_slots, normed_b, stream_b,
-    load_sem, halo_sem, send_sem, recv_sem, power_sem, store_sem,
+    gate_t, skip_t, res_t, flat, spectrum_h, product, power_slots,
+    load_sem, halo_sem, send_sem, recv_sem, power_sem,
 ):
     me, ch = lax.axis_index("seq"), lax.axis_index("ch")
     tokens, channels = h_b.shape
@@ -75,19 +75,10 @@
         y = lax.rem(lax.rem(me, line) + order(lax.rem(step, line), line), line)
         return z * line + y
 
-    barrier = pltpu.get_barrier_semaphore()
-
-    def greet(step, _):
-        pl.semaphore_signal(barrier, inc=1, device_id=(peer(step), ch), device_id_type=MESH)
-        return 0
-
-    lax.fori_loop(0, pieces - 1, greet, 0)
-
-    def greet_row(d, _):
-        pl.semaphore_signal(barrier, inc=1, device_id=(me, lax.rem(ch + d, groups)), device_id_type=MESH)
-        return 0
-
-    lax.fori_loop(1, groups, greet_row, 0)
+    def early(step):
+        z = lax.rem(step // line, 2) * (rings // 2) + step // (2 * line)
+        y = lax.rem(lax.rem(me, line) + order(lax.rem(step, line), line), line)
+        return z * line + y
 
     pairs = [
         (h_in, h_b), (q_in, q_b), (k_in, k_b), (v_in, v_b), (taps_in, taps), (bias_in, bias), (first_in, first),
@@ -95,11 +86,28 @@
         (res_in, res_b), (gain_in, gain),
     ]
     loads = [pltpu.make_async_copy(src, dst, load_sem.at[i]) for i, (src, dst) in enumerate(pairs)]
-    for load in loads:
+    for load in loads[:4]:
         load.start()
+
+    barrier = pltpu.get_barrier_semaphore()
+
+    def greet(step, _):
+        pl.semaphore_signal(barrier, inc=1, device_id=(peer(step), ch), device_id_type=MESH)
+        return 0
+
+    lax.fori_loop(0, pieces - 1, greet, 0)
+
+    def greet_row(d, _):
+        pl.semaphore_signal(barrier, inc=1, device_id=(me, lax.rem(ch + d, groups)), device_id_type=MESH)
+        return 0
+
+    lax.fori_loop(1, groups, greet_row, 0)
 
     def tile(r, c):
         return slice(r * LANES, (r + 1) * LANES), slice(c * LANES, (c + 1) * LANES)
+
+    for load in loads[4:]:
+        load.start()
 
     loads[0].wait()
     for r in range(blocks):
@@ -123,18 +131,22 @@
     def _():
         halo_copy.start()
 
-    def send_all(source, target, slot):
+    def send_all(source, target, slot, partner=peer):
         def send(step, _):
-            other = peer(step)
-            pltpu.make_async_remote_copy(
-                src_ref=source.at[pl.ds(pl.multiple_of(other * own, own), own)],
-                dst_ref=target.at[pl.ds(pl.multiple_of(me * own, own), own)],
-                send_sem=send_sem.at[slot], recv_sem=recv_sem.at[slot],
-                device_id=(other, ch), device_id_type=MESH,
-            ).start()
+            other = partner(step)
+
+            @pl.when(other != me)
+            def _():
+                pltpu.make_async_remote_copy(
+                    src_ref=source.at[pl.ds(pl.multiple_of(other * own, own), own)],
+                    dst_ref=target.at[pl.ds(pl.multiple_of(me * own, own), own)],
+                    send_sem=send_sem.at[slot], recv_sem=recv_sem.at[slot],
+                    device_id=(other, ch), device_id_type=MESH,
+                ).start()
+
             return 0
 
-        lax.fori_loop(0, pieces - 1, send, 0)
+        lax.fori_loop(0, pieces, send, 0)
         mine = pl.ds(pl.multiple_of(me * own, own), own)
         pltpu.make_async_copy(source.at[mine], target.at[mine], recv_sem.at[slot]).start()
 
@@ -282,7 +294,7 @@
             return 0
 
         lax.fori_loop(0, channels // 64, narrow, 0)
-        send_all(y_send.at[part], y_recv.at[part], 3 + part)
+        send_all(y_send.at[part], y_recv.at[part], 3 + part, early if part else peer)
 
     total = jnp.zeros((8, tokens), F32)
     for part in range(2):
@@ -315,8 +327,6 @@
         for c in range(wide):
             rows, cols = tile(r, c)
             stream_b[rows, cols] = res_t[cols, rows].T.astype(BF16)
-    stream_copy = pltpu.make_async_copy(stream_b, stream_out, store_sem.at[0])
-    stream_copy.start()
 
     part = power_slots.at[pl.ds(0, groups - 1)]
     pltpu.make_async_copy(part, part, power_sem.at[1]).wait()
@@ -328,16 +338,12 @@
         for c in range(wide):
             cols = tile(r, c)[1]
             normed_b[rows, cols] = (stream_b[rows, cols].astype(F32) * column * gain[0:1, cols]).astype(BF16)
-    normed_copy = pltpu.make_async_copy(normed_b, normed_out, store_sem.at[1])
-    normed_copy.start()
 
     pltpu.make_async_copy(part, part, power_sem.at[0]).wait()
     wait_send(h_send, 0)
     for part in range(2):
         wait_send(z_send.at[part], 1 + part)
         wait_send(y_send.at[part], 3 + part)
-    stream_copy.wait()
-    normed_copy.wait()
 
 
 def per_device(constants, q_proj, k_proj, v_proj, short_weight, long_filter, long_bias, residual, norm_gain):
@@ -362,19 +368,18 @@
         pltpu.VMEM((own * LANES, 2 * LANES), F32),
         pltpu.VMEM((tokens // LANES // 2, channels, LANES), F32),
         pltpu.VMEM((groups, 1, tokens), F32),
-        pltpu.VMEM(block, BF16),
-        pltpu.VMEM(block, BF16),
     ]
-    scratch += [pltpu.SemaphoreType.DMA((count,)) for count in (14, 2, 5, 5, 2, 2)]
+    scratch += [pltpu.SemaphoreType.DMA((count,)) for count in (14, 2, 5, 5, 2)]
     anywhere = pl.BlockSpec(memory_space=pl.ANY)
+    operands = tuple(pltpu.with_memory_space_constraint(x, pltpu.HBM) for x in operands)
     return pl.pallas_call(
         functools.partial(kernel, pieces, groups),
         out_shape=(jax.ShapeDtypeStruct(block, BF16),) * 2,
         in_specs=[anywhere] * len(operands),
-        out_specs=(anywhere,) * 2,
+        out_specs=(pl.BlockSpec(memory_space=pltpu.VMEM),) * 2,
         scratch_shapes=scratch,
         compiler_params=pltpu.CompilerParams(
-            collective_id=0, has_side_effects=True, vmem_limit_bytes=62 * 2**20
+            collective_id=0, has_side_effects=True, vmem_limit_bytes=32 * 2**20
         ),
         cost_estimate=pl.CostEstimate(flops=1_300_000_000, bytes_accessed=4_000_000, transcendentals=0),
     )(*operands)

time: 56.9 us -> 53.7 us (0.944)
  Pallas kernels: 53.4 us -> 51.4 us
  local copies, waits for them, and re-layouts: 2.72 us -> 1.59 us
    pallas_call x1, Pallas kernels: 53.4 us -> 51.4 us  [per_device(): pl.pallas_call(functools.partial(kernel, pieces, groups), out_shape=(jax....]
    unnamed x4 -> x2, local copies, waits for them, and re-layouts: 2.72 us -> 1.59 us
where the time goes in v2:
time: 53.7 us; the launch traced here: 53.6 us
  Pallas kernels  51.4 us (96%)
  local copies, waits for them, and re-layouts  1.59 us (3%)
  between operations  0.64 us (1%)
    pallas_call x1, Pallas kernels, per_device(): pl.pallas_call(functools.partial(kernel, pieces, groups), out_shape=(jax....  51.4 us
    unnamed x2, local copies, waits for them, and re-layouts  1.59 us

profile of v2, /device:TPU:1, one launch (start us, length us, event | category | flops | bytes accessed | tf_op | source)
XLA Modules:
  0.0 53.6 jit_solution(16409059978241366025)
XLA Ops:
  0.6 51.4 %shard_map.149 = (bf16[512,512]{1,0:T(8,128)(2,1)S(1)}, bf16[512,512]{1,0:T(8,128)(2,1)S(1)}) custom-call(bf16[512,512]{1,0:T(8,128)(2,1)} %q_in.1, bf16[512,512]{1,0:T(8,128)(2,1)} %k_in.1, bf16[512,512]{1,0:T(8,128)(2,1)} %v_in.1, bf16[512,512]{1,0:T(8,128)(2,1)} %h_in.1, bf16[512,512]{1,0:T(8,128)(2,1)} %res_in.1, f32[3,3,512]{2,1,0:T(4,128)} %taps_in.1, ...), custom_call_target="tpu_custom_call" | custom-call | flops 1300000000 | bytes 4000000 | tf_op jit(solution)/shard_map/pallas_call | solution.py:375
  52.0 0.8 %copy.18 = bf16[512,512]{1,0:T(8,128)(2,1)} copy(bf16[512,512]{1,0:T(8,128)(2,1)S(1)} %get-tuple-element.4) | data formatting | bytes 1048576
  52.8 0.8 %copy.19 = bf16[512,512]{1,0:T(8,128)(2,1)} copy(bf16[512,512]{1,0:T(8,128)(2,1)S(1)} %get-tuple-element.5) | data formatting | bytes 1048576

commit v3 on v2

--- a/solution.py
+++ b/solution.py
@@ -54,7 +54,7 @@
     groups,
     q_in, k_in, v_in, h_in, res_in, taps_in, bias_in, gain_in,
     first_in, second_in, third_in, last_in, cos_in, sin_in,
-    stream_b, normed_b,
+    both,
     q_b, k_b, v_b, h_b, res_b, taps, bias, gain,
     first, second, third, last, cos_t, sin_t,
     pad_q, pad_k, pad_v, halo_out, halo_in,
@@ -234,7 +234,7 @@
                 flat[i, rows, :] = received[rows, i * LANES : (i + 1) * LANES].astype(F32)
             return 0
 
-        lax.fori_loop(0, channels // 64, step, 0)
+        lax.fori_loop(0, channels // 64, step, 0, unroll=4)
 
     wait_recv(h_recv, 0)
     widen(h_recv, blocks)
@@ -247,7 +247,7 @@
         spectrum_h[pl.ds(pl.multiple_of(p * 256, 256), 256), :] = forward(signal)
         return 0
 
-    lax.fori_loop(0, own // 2, filter_step, 0)
+    lax.fori_loop(0, own // 2, filter_step, 0, unroll=4)
 
     for part in range(2):
         wait_recv(z_recv.at[part], 1 + part)
@@ -285,7 +285,7 @@
                     ]
             return 0
 
-        lax.fori_loop(0, own // 4, signal_step, 0, unroll=2)
+        lax.fori_loop(0, own // 4, signal_step, 0, unroll=4)
 
         def narrow(r, _):
             rows = pl.ds(pl.multiple_of(r * 64, 64), 64)
@@ -293,7 +293,7 @@
                 y_send[part, rows, i * LANES : (i + 1) * LANES] = product[i, rows, :].astype(BF16)
             return 0
 
-        lax.fori_loop(0, channels // 64, narrow, 0)
+        lax.fori_loop(0, channels // 64, narrow, 0, unroll=4)
         send_all(y_send.at[part], y_recv.at[part], 3 + part, early if part else peer)
 
     total = jnp.zeros((8, tokens), F32)
@@ -309,7 +309,7 @@
             res_t[rows, :] = stream
             return total + stream * stream
 
-        total = lax.fori_loop(0, pieces, gate_step, total, unroll=4)
+        total = lax.fori_loop(0, pieces, gate_step, total, unroll=8)
     power_slots[ch] = jnp.sum(total, axis=0, keepdims=True)
 
     def power_copy(d):
@@ -320,13 +320,13 @@
             device_id=(me, other), device_id_type=MESH,
         )
 
-    for d in range(1, groups):
+    for d in (4, 3, 5, 2, 6, 7, 1):
         power_copy(d).start()
 
     for r in range(blocks):
         for c in range(wide):
             rows, cols = tile(r, c)
-            stream_b[rows, cols] = res_t[cols, rows].T.astype(BF16)
+            both[0, rows, cols] = res_t[cols, rows].T.astype(BF16)
 
     part = power_slots.at[pl.ds(0, groups - 1)]
     pltpu.make_async_copy(part, part, power_sem.at[1]).wait()
@@ -337,7 +337,7 @@
         column = jnp.broadcast_to(scale[:, rows], (LANES, LANES)).T
         for c in range(wide):
             cols = tile(r, c)[1]
-            normed_b[rows, cols] = (stream_b[rows, cols].astype(F32) * column * gain[0:1, cols]).astype(BF16)
+            both[1, rows, cols] = (both[0, rows, cols].astype(F32) * column * gain[0:1, cols]).astype(BF16)
 
     pltpu.make_async_copy(part, part, power_sem.at[0]).wait()
     wait_send(h_send, 0)
@@ -372,17 +372,18 @@
     scratch += [pltpu.SemaphoreType.DMA((count,)) for count in (14, 2, 5, 5, 2)]
     anywhere = pl.BlockSpec(memory_space=pl.ANY)
     operands = tuple(pltpu.with_memory_space_constraint(x, pltpu.HBM) for x in operands)
-    return pl.pallas_call(
+    both = pl.pallas_call(
         functools.partial(kernel, pieces, groups),
-        out_shape=(jax.ShapeDtypeStruct(block, BF16),) * 2,
+        out_shape=jax.ShapeDtypeStruct((2, *block), BF16),
         in_specs=[anywhere] * len(operands),
-        out_specs=(pl.BlockSpec(memory_space=pltpu.VMEM),) * 2,
+        out_specs=pl.BlockSpec(memory_space=pltpu.VMEM),
         scratch_shapes=scratch,
         compiler_params=pltpu.CompilerParams(
             collective_id=0, has_side_effects=True, vmem_limit_bytes=32 * 2**20
         ),
         cost_estimate=pl.CostEstimate(flops=1_300_000_000, bytes_accessed=4_000_000, transcendentals=0),
     )(*operands)
+    return both[0], both[1]
 
 
 def solution(mesh):

time: 53.7 us -> 53 us (0.987)
  local copies, waits for them, and re-layouts: 1.59 us -> 1.03 us
    unnamed x2 -> x0, local copies, waits for them, and re-layouts: 1.59 us -> none
    squeeze x0 -> x1, local copies, waits for them, and re-layouts: none -> 1.03 us  [per_device(): return (both[0], both[1])]
where the time goes in v3:
time: 53 us; the launch traced here: 52.9 us
  Pallas kernels  51.2 us (97%)
  local copies, waits for them, and re-layouts  1.03 us (2%)
  between operations  0.64 us (1%)
    pallas_call x1, Pallas kernels, per_device(): pl.pallas_call(functools.partial(kernel, pieces, groups), out_shape=jax.S...  51.2 us

profile of v3, /device:TPU:1, one launch (start us, length us, event | category | flops | bytes accessed | tf_op | source)
XLA Modules:
  0.0 52.9 jit_solution(13589445612824962982)
XLA Ops:
  0.6 51.2 %shard_map.149 = bf16[2,512,512]{2,1,0:T(8,128)(2,1)S(1)} custom-call(bf16[512,512]{1,0:T(8,128)(2,1)} %q_in.1, bf16[512,512]{1,0:T(8,128)(2,1)} %k_in.1, bf16[512,512]{1,0:T(8,128)(2,1)} %v_in.1, bf16[512,512]{1,0:T(8,128)(2,1)} %h_in.1, bf16[512,512]{1,0:T(8,128)(2,1)} %res_in.1, f32[3,3,512]{2,1,0:T(4,128)} %taps_in.1, f32[1,512]{1,0:T(1,128)} %bitcast.6, ...), custom_call_target="tpu_custom_call" | custom-call | flops 1300000000 | bytes 4000000 | tf_op jit(solution)/shard_map/pallas_call | solution.py:375
  51.8 1.0 %slice_bitcast_fusion = (bf16[512,512]{1,0:T(8,128)(2,1)}, bf16[512,512]{1,0:T(8,128)(2,1)}) fusion(bf16[2,512,512]{2,1,0:T(8,128)(2,1)S(1)} %shard_map.149), kind=kLoop, calls=%fused_computation | loop fusion | bytes 2097152 | tf_op jit(solution)/shard_map/squeeze | solution.py:386

commit v4 on v3

--- a/solution.py
+++ b/solution.py
@@ -31,10 +31,10 @@
     second = np.block([[cosine, -sine], [sine, cosine]])
     angle = 2 * math.pi / (n * n) * (quarter[:, None] * points[None, :])
     return (
-        first.astype(ml_dtypes.bfloat16),
-        second.astype(ml_dtypes.bfloat16),
-        second.T.copy().astype(ml_dtypes.bfloat16),
-        last.astype(ml_dtypes.bfloat16),
+        np.concatenate(halves(first), axis=1),
+        np.stack(halves(second)),
+        np.stack(halves(second.T.copy())),
+        np.stack(halves(last)),
         np.cos(angle).astype(np.float32),
         np.sin(angle).astype(np.float32),
     )
@@ -42,6 +42,16 @@
 
 def dot(left, right):
     return jnp.dot(left, right, preferred_element_type=F32)
+
+
+def split(x):
+    high = x.astype(BF16)
+    return high, (x - high.astype(F32)).astype(BF16)
+
+
+def halves(table):
+    high = table.astype(ml_dtypes.bfloat16)
+    return high, (table - high.astype(np.float64)).astype(ml_dtypes.bfloat16)
 
 
 def order(step, count):
@@ -77,7 +87,7 @@
 
     def early(step):
         z = lax.rem(step // line, 2) * (rings // 2) + step // (2 * line)
-        y = lax.rem(lax.rem(me, line) + order(lax.rem(step, line), line), line)
+        y = lax.rem(step, line)
         return z * line + y
 
     pairs = [
@@ -201,8 +211,7 @@
                     jnp.stack([x[:, part] for x in parts], axis=1).reshape(LANES, LANES).astype(BF16)
                 )
 
-    for part in range(2):
-        send_all(z_send.at[part], z_recv.at[part], 1 + part)
+    send_all(z_send.at[0], z_recv.at[0], 1)
 
     loads[12].wait()
     for r in range(blocks):
@@ -215,17 +224,22 @@
     for i in (6, 7, 8, 9, 10, 11, 13):
         loads[i].wait()
 
+    def product_of(x, table):
+        high, low = split(x)
+        return dot(high, table[0]) + (dot(low, table[0]) + dot(high, table[1]))
+
     def forward(signal):
-        partial = dot(first[...], jnp.concatenate(signal, axis=1).astype(BF16))
+        signal = jnp.concatenate(signal, axis=1).astype(BF16)
+        partial = dot(first[...], jnp.concatenate([signal, signal], axis=0))
         turned = []
         for e in range(2):
             real = partial[:LANES, e * LANES : (e + 1) * LANES]
             imag = partial[LANES:, e * LANES : (e + 1) * LANES]
             cosine, sine = cos_t[...], sin_t[...]
             turned.append(
-                jnp.concatenate([real * cosine + imag * sine, imag * cosine - real * sine], axis=1).astype(BF16)
+                jnp.concatenate([real * cosine + imag * sine, imag * cosine - real * sine], axis=1)
             )
-        return dot(jnp.concatenate(turned, axis=0), second[...])
+        return product_of(jnp.concatenate(turned, axis=0), second)
 
     def widen(received, count):
         def step(r, _):
@@ -248,6 +262,9 @@
         return 0
 
     lax.fori_loop(0, own // 2, filter_step, 0, unroll=4)
+
+    wait_send(z_send.at[0], 1)
+    send_all(z_send.at[1], z_recv.at[1], 2)
 
     for part in range(2):
         wait_recv(z_recv.at[part], 1 + part)
@@ -267,17 +284,18 @@
             x = forward(signal)
             w = spectrum_h[pl.ds(pl.multiple_of((part * own // 4 + p) * 256, 256), 256), :]
             xr, xi, wr, wi = x[:, :LANES], x[:, LANES:], w[:, :LANES], w[:, LANES:]
-            both = jnp.concatenate([xr * wr - xi * wi, xr * wi + xi * wr], axis=1).astype(BF16)
-            back = dot(both, third[...])
+            both = jnp.concatenate([xr * wr - xi * wi, xr * wi + xi * wr], axis=1)
+            back = product_of(both, third)
             turned = []
             for e in range(2):
                 real = back[e * LANES : (e + 1) * LANES, :LANES]
                 imag = back[e * LANES : (e + 1) * LANES, LANES:]
                 cosine, sine = cos_t[...], sin_t[...]
                 turned.append(
-                    jnp.concatenate([real * cosine - imag * sine, real * sine + imag * cosine], axis=0).astype(BF16)
+                    jnp.concatenate([real * cosine - imag * sine, real * sine + imag * cosine], axis=0)
                 )
-            result = dot(last[...], jnp.concatenate(turned, axis=1))
+            high, low = split(jnp.concatenate(turned, axis=1))
+            result = dot(last[0], high) + (dot(last[0], low) + dot(last[1], high))
             for e in range(2):
                 for i in range(blocks):
                     product[i % half, pl.ds((i // half) * (own // 2) + 2 * p + e, pieces, stride=own), :] = result[
@@ -341,8 +359,8 @@
 
     pltpu.make_async_copy(part, part, power_sem.at[0]).wait()
     wait_send(h_send, 0)
+    wait_send(z_send.at[1], 2)
     for part in range(2):
-        wait_send(z_send.at[part], 1 + part)
         wait_send(y_send.at[part], 3 + part)
 
 

time: 53 us -> 52.9 us (level)
  no operation moved by 1% of the time
where the time goes in v4:
time: 52.9 us; the launch traced here: 52.8 us
  Pallas kernels  51.1 us (97%)
  local copies, waits for them, and re-layouts  1.03 us (2%)
  between operations  0.64 us (1%)
    pallas_call x1, Pallas kernels, per_device(): pl.pallas_call(functools.partial(kernel, pieces, groups), out_shape=jax.S...  51.1 us

profile of v4, /device:TPU:1, one launch (start us, length us, event | category | flops | bytes accessed | tf_op | source)
XLA Modules:
  0.0 52.8 jit_solution(18227799085990588212)
XLA Ops:
  0.6 51.1 %shard_map.149 = bf16[2,512,512]{2,1,0:T(8,128)(2,1)S(1)} custom-call(bf16[512,512]{1,0:T(8,128)(2,1)} %q_in.1, bf16[512,512]{1,0:T(8,128)(2,1)} %k_in.1, bf16[512,512]{1,0:T(8,128)(2,1)} %v_in.1, bf16[512,512]{1,0:T(8,128)(2,1)} %h_in.1, bf16[512,512]{1,0:T(8,128)(2,1)} %res_in.1, f32[3,3,512]{2,1,0:T(4,128)} %taps_in.1, f32[1,512]{1,0:T(1,128)} %bitcast.6, ...), custom_call_target="tpu_custom_call" | custom-call | flops 1300000000 | bytes 4000000 | tf_op jit(solution)/shard_map/pallas_call | solution.py:393
  51.8 1.0 %slice_bitcast_fusion = (bf16[512,512]{1,0:T(8,128)(2,1)}, bf16[512,512]{1,0:T(8,128)(2,1)}) fusion(bf16[2,512,512]{2,1,0:T(8,128)(2,1)S(1)} %shard_map.149), kind=kLoop, calls=%fused_computation | loop fusion | bytes 2097152 | tf_op jit(solution)/shard_map/squeeze | solution.py:404

commit v5 on v4

--- a/solution.py
+++ b/solution.py
@@ -96,13 +96,13 @@
         (res_in, res_b), (gain_in, gain),
     ]
     loads = [pltpu.make_async_copy(src, dst, load_sem.at[i]) for i, (src, dst) in enumerate(pairs)]
-    for load in loads[:4]:
-        load.start()
 
     barrier = pltpu.get_barrier_semaphore()
 
     def greet(step, _):
-        pl.semaphore_signal(barrier, inc=1, device_id=(peer(step), ch), device_id_type=MESH)
+        pl.semaphore_signal(
+            barrier, inc=1, device_id=(step + jnp.where(step >= me, 1, 0), ch), device_id_type=MESH
+        )
         return 0
 
     lax.fori_loop(0, pieces - 1, greet, 0)
@@ -116,7 +116,7 @@
     def tile(r, c):
         return slice(r * LANES, (r + 1) * LANES), slice(c * LANES, (c + 1) * LANES)
 
-    for load in loads[4:]:
+    for load in loads:
         load.start()
 
     loads[0].wait()

time: 52.9 us -> 52.7 us (level)
  no operation moved by 1% of the time
where the time goes in v5:
time: 52.7 us; the launch traced here: 52.4 us
  Pallas kernels  50.8 us (96%)
  local copies, waits for them, and re-layouts  1.03 us (2%)
  between operations  0.64 us (1%)
    pallas_call x1, Pallas kernels, per_device(): pl.pallas_call(functools.partial(kernel, pieces, groups), out_shape=jax.S...  50.8 us

profile of v5, /device:TPU:1, one launch (start us, length us, event | category | flops | bytes accessed | tf_op | source)
XLA Modules:
  0.0 52.4 jit_solution(11601185660122769032)
XLA Ops:
  0.6 50.8 %shard_map.149 = bf16[2,512,512]{2,1,0:T(8,128)(2,1)S(1)} custom-call(bf16[512,512]{1,0:T(8,128)(2,1)} %q_in.1, bf16[512,512]{1,0:T(8,128)(2,1)} %k_in.1, bf16[512,512]{1,0:T(8,128)(2,1)} %v_in.1, bf16[512,512]{1,0:T(8,128)(2,1)} %h_in.1, bf16[512,512]{1,0:T(8,128)(2,1)} %res_in.1, f32[3,3,512]{2,1,0:T(4,128)} %taps_in.1, f32[1,512]{1,0:T(1,128)} %bitcast.6, ...), custom_call_target="tpu_custom_call" | custom-call | flops 1300000000 | bytes 4000000 | tf_op jit(solution)/shard_map/pallas_call | solution.py:393
  51.4 1.0 %slice_bitcast_fusion = (bf16[512,512]{1,0:T(8,128)(2,1)}, bf16[512,512]{1,0:T(8,128)(2,1)}) fusion(bf16[2,512,512]{2,1,0:T(8,128)(2,1)S(1)} %shard_map.149), kind=kLoop, calls=%fused_computation | loop fusion | bytes 2097152 | tf_op jit(solution)/shard_map/squeeze | solution.py:404

commit v6 on v5

--- a/solution.py
+++ b/solution.py
@@ -382,9 +382,9 @@
     scratch += [pltpu.VMEM(block, BF16)]
     scratch += [pltpu.VMEM((channels, tokens), F32) for _ in range(3)]
     scratch += [
-        pltpu.VMEM((tokens // LANES, channels, LANES), F32),
+        pltpu.VMEM((tokens // LANES, channels + own, LANES), F32),
         pltpu.VMEM((own * LANES, 2 * LANES), F32),
-        pltpu.VMEM((tokens // LANES // 2, channels, LANES), F32),
+        pltpu.VMEM((tokens // LANES // 2, channels + own, LANES), F32),
         pltpu.VMEM((groups, 1, tokens), F32),
     ]
     scratch += [pltpu.SemaphoreType.DMA((count,)) for count in (14, 2, 5, 5, 2)]

time: 52.7 us -> 52.7 us (level)
  no operation moved by 1% of the time
where the time goes in v6:
time: 52.7 us; the launch traced here: 52.4 us
  Pallas kernels  50.8 us (96%)
  local copies, waits for them, and re-layouts  1.03 us (2%)
  between operations  0.64 us (1%)
    pallas_call x1, Pallas kernels, per_device(): pl.pallas_call(functools.partial(kernel, pieces, groups), out_shape=jax.S...  50.8 us

profile of v6, /device:TPU:1, one launch (start us, length us, event | category | flops | bytes accessed | tf_op | source)
XLA Modules:
  0.0 52.4 jit_solution(9694341410507401527)
XLA Ops:
  0.6 50.8 %shard_map.149 = bf16[2,512,512]{2,1,0:T(8,128)(2,1)S(1)} custom-call(bf16[512,512]{1,0:T(8,128)(2,1)} %q_in.1, bf16[512,512]{1,0:T(8,128)(2,1)} %k_in.1, bf16[512,512]{1,0:T(8,128)(2,1)} %v_in.1, bf16[512,512]{1,0:T(8,128)(2,1)} %h_in.1, bf16[512,512]{1,0:T(8,128)(2,1)} %res_in.1, f32[3,3,512]{2,1,0:T(4,128)} %taps_in.1, f32[1,512]{1,0:T(1,128)} %bitcast.6, ...), custom_call_target="tpu_custom_call" | custom-call | flops 1300000000 | bytes 4000000 | tf_op jit(solution)/shard_map/pallas_call | solution.py:393
  51.4 1.0 %slice_bitcast_fusion = (bf16[512,512]{1,0:T(8,128)(2,1)}, bf16[512,512]{1,0:T(8,128)(2,1)}) fusion(bf16[2,512,512]{2,1,0:T(8,128)(2,1)S(1)} %shard_map.149), kind=kLoop, calls=%fused_computation | loop fusion | bytes 2097152 | tf_op jit(solution)/shard_map/squeeze | solution.py:404
